TPU v7x, 32 devices: a whole 2x2x4 slice. The times are simulated.
32 devices in a mesh: dp: 4 (over y, x), tensor: 8 (over z, core).
Axes of the slice: x: 2, y: 2, z: 4, core: 2. Of those that a mesh axis runs over, the one named last changes fastest.
Arguments:
- inputs: bfloat16 [1024, 28672], P('dp', 'tensor'), may hold values from -0.1875 to 0.1875
- output_gradient: bfloat16 [1024, 8192], P('dp', 'tensor'), may hold values from -6 to 6
- frozen: bfloat16 [8192, 28672], P('dp', 'tensor'), may hold values from -0.5905695 to 0.5905695
- adapter_down_factor: bfloat16 [64, 28672], P(None, 'tensor'), may hold values from -0.03125 to 0.03125
- adapter_up_factor: bfloat16 [8192, 64], P('dp'), may hold values from -0.3125 to 0.3125
- magnitude: float32 [8192], P('dp'), may hold values from 0.5 to 2
Outputs:
- input_gradient_rows: bfloat16 [1024, 28672], P('dp', 'tensor')
- adapter_down_gradient: float32 [64, 28672], P(None, 'tensor')
- adapter_up_gradient: float32 [8192, 64], P('dp')
- magnitude_gradient: float32 [8192], P('dp')
All inputs are finite; a program needn't handle non-finite values.
Results may differ from a plain program's by a relative error of at most 0.0057.
Values may be sent and summed in bfloat16 or wider, within the bound.
A program may use at most 192 MiB of HBM per device.

v0:
```python
import jax
import jax.numpy as jnp
from jax import lax
from jax.sharding import PartitionSpec as P

adapter_scale = 2.0
epsilon = 1e-06


def local(inputs, output_gradient, frozen, adapter_down_factor, adapter_up_factor, magnitude):
    full_grad = lax.all_gather(output_gradient, "tensor", axis=1, tiled=True)
    row_grad = lax.all_to_all(full_grad, "dp", split_axis=1, concat_axis=0, tiled=True)
    combined_weight = frozen.astype(jnp.float32) + adapter_scale * jnp.dot(
        adapter_up_factor, adapter_down_factor, preferred_element_type=jnp.float32
    )
    merged_b = combined_weight.astype(jnp.bfloat16)
    squares = jnp.sum(combined_weight * combined_weight, axis=1)
    total_squares = lax.psum(squares, "tensor")
    weight_row_norm = jnp.sqrt(total_squares + epsilon)
    col_scale = magnitude / weight_row_norm
    scaled_rows = (row_grad.astype(jnp.float32) * col_scale[None, :]).astype(jnp.bfloat16)
    summed = lax.psum_scatter(
        jnp.dot(scaled_rows, merged_b, preferred_element_type=jnp.float32),
        "dp",
        scatter_dimension=0,
        tiled=True,
    )
    input_gradient_rows = summed.astype(jnp.bfloat16)
    product = lax.dot_general(
        row_grad,
        lax.all_gather(inputs, "dp", axis=0, tiled=True),
        (((0,), (0,)), ((), ())),
        preferred_element_type=jnp.float32,
    )
    gradient_row_sums = lax.psum(jnp.sum(product * combined_weight, axis=1), "tensor")
    combined_weight_gradient = col_scale[:, None] * product
    down_partial_sum = adapter_scale * lax.dot_general(
        adapter_up_factor.astype(jnp.float32),
        combined_weight_gradient,
        (((0,), (0,)), ((), ())),
        precision=lax.Precision.HIGHEST,
    )
    adapter_down_gradient = lax.psum(down_partial_sum, "dp")
    up_partial_sum = adapter_scale * jnp.dot(
        combined_weight_gradient,
        adapter_down_factor.astype(jnp.float32).T,
        precision=lax.Precision.HIGHEST,
    )
    adapter_up_gradient = lax.psum(up_partial_sum, "tensor")
    magnitude_gradient = gradient_row_sums / weight_row_norm
    return (input_gradient_rows, adapter_down_gradient, adapter_up_gradient, magnitude_gradient)


def solution(mesh):
    placed = (
        P("dp", "tensor"),
        P("dp", "tensor"),
        P("dp", "tensor"),
        P(None, "tensor"),
        P("dp", None),
        P("dp"),
    )
    return jax.shard_map(
        local,
        mesh=mesh,
        in_specs=placed,
        out_specs=(P("dp", "tensor"), P(None, "tensor"), P("dp", None), P("dp")),
        check_vma=False,
    )
```

profile of v0, /device:TPU:24, one launch (start us, length us, event | category | flops | bytes accessed | tf_op | source)
XLA Modules:
  0.0 517.4 jit_solution(6912844076964576439)
XLA Ops:
  7.2 0.0 copy-start
  7.2 0.0 all-gather.3.cloned.1.call-start
  7.2 2.1 copy.10
  9.3 0.0 all-gather.3.cloned.1.call-update
  9.3 0.0 all-gather.5.cloned.1.call-start
  9.4 0.7 all-gather.5.cloned.1.call-update
  10.1 46.1 %all-gather.3.cloned.1.call-done = bf16[256,8192]{0,1:T(8,128)(2,1)} async-done(((bf16[256,1024]{0,1:T(8,128)(2,1)}), bf16[256,8192]{0,1:T(8,128)(2,1)}) %all-gather.3.cloned.1.call-update) | async-done | bytes 4194320 | tf_op jit(solution)/shard_map/all_gather | solution.py:11
  56.2 4.8 all-to-all-start
  61.0 0.0 reduce-scatter.2.cloned.1.call-start
  61.1 0.0 copy-done
  61.1 15.8 %multiply_add_fusion = f32[2048,3584]{1,0:T(8,128)} fusion(bf16[2048,3584]{1,0:T(8,128)(2,1)} %param.8, bf16[2048,64]{0,1:T(8,128)(2,1)} %param.10, bf16[64,3584]{1,0:T(8,128)(2,1)S(1)} %copy-done), kind=kOutput, calls=%fused_computation.2 | convolution fusion | flops 961544192 | bytes 44761088 | tf_op jit(solution)/shard_map/dot_general | solution.py:13
  76.9 51.9 %all-to-all-done = bf16[256,4,2048]{0,2,1:T(8,128)(2,1)} async-done(((bf16[256,4,2048]{0,2,1:T(8,128)(2,1)}), bf16[256,4,2048]{0,2,1:T(8,128)(2,1)}, u32[]{:S(2)}, u32[]{:S(2)}) %all-to-all-start) | async-done | bytes 4194336 | tf_op jit(solution)/shard_map/all_to_all | solution.py:12
  128.8 6.3 %copy.11 = bf16[4,256,2048]{2,1,0:T(8,128)(2,1)} copy(bf16[4,256,2048]{1,2,0:T(8,128)(2,1)} %bitcast.1) | data formatting | bytes 8388608 | tf_op jit(solution)/shard_map/all_to_all | solution.py:12
  135.0 40.8 %all-gather.5.cloned.1.call-done = bf16[1024,3584]{1,0:T(8,128)(2,1)} async-done(((bf16[256,3584]{1,0:T(8,128)(2,1)}), bf16[1024,3584]{1,0:T(8,128)(2,1)}) %all-gather.5.cloned.1.call-update) | async-done | bytes 7340048 | tf_op jit(solution)/shard_map/all_gather | solution.py:31
  175.9 0.0 copy-start.2
  175.9 29.3 %multiply_reduce_fusion = (f32[2048]{0:T(1024)S(1)}, f32[2048]{0:T(1024)S(1)}, f32[2048,3584]{1,0:T(8,128)}) fusion(f32[2048,3584]{1,0:T(8,128)} %multiply_add_fusion, bf16[1024,2048]{1,0:T(8,128)(2,1)} %bitcast.12, bf16[1024,3584]{1,0:T(8,128)(2,1)} %all-gather.5.cloned.1.call-done), kind=kOutput, calls=%fused_computation | convolution fusion | flops 15061741568 | bytes 70270976 | tf_op jit(solution)/shard_map/dot_general | solution.py:29
  205.2 23.2 %all-reduce = (f32[2048]{0:T(1024)S(1)}, f32[2048]{0:T(1024)S(1)}) all-reduce(f32[2048]{0:T(1024)S(1)} %get-tuple-element.5, f32[2048]{0:T(1024)S(1)} %get-tuple-element.4), channel_id=1, replica_groups=mesh['dp'=4,'tensor'=8] {'tensor'}, use_global_device_ids=true, to_apply=%region_1.0 | all-reduce | flops 4096 | bytes 32768 | tf_op jit(solution)/shard_map/psum | solution.py:18
  228.3 0.0 copy-done.2
  228.4 0.6 fusion.18
  229.0 24.8 %fusion.6 = f32[1024,3584]{1,0:T(8,128)} fusion(f32[2048,3584]{1,0:T(8,128)} %multiply_add_fusion, bf16[1024,2048]{1,0:T(8,128)(2,1)} %bitcast.13, f32[2048]{0:T(1024)S(1)} %get-tuple-element.9), kind=kOutput, calls=%fused_computation.9 | convolution fusion | flops 15046017024 | bytes 48242688 | tf_op jit(solution)/shard_map/dot_general | solution.py:23
  253.8 0.0 reduce-scatter.2.cloned.1.call-update
  253.8 0.0 all-reduce.6.cloned.1.call-start
  253.8 0.0 copy-start.1
  253.9 21.0 %fusion.15 = f32[2048,64]{0,1:T(8,128)} fusion(bf16[64,3584]{1,0:T(8,128)(2,1)S(1)} %copy-done, f32[2048,3584]{1,0:T(8,128)} %get-tuple-element.10, f32[2048]{0:T(1024)S(1)} %get-tuple-element.9), kind=kOutput, calls=%fused_computation.15 | convolution fusion | flops 5644615680 | bytes 30351360 | tf_op jit(solution)/shard_map/dot_general | solution.py:44
  274.9 0.0 all-reduce.6.cloned.1.call-update
  274.9 0.3 all-reduce.4.cloned.1.call-start
  275.2 0.0 copy-done.1
  275.2 17.7 %fusion.11 = f32[64,3584]{1,0:T(8,128)} fusion(bf16[2048,64]{0,1:T(8,128)(2,1)S(1)} %copy-done.1, f32[2048,3584]{1,0:T(8,128)} %get-tuple-element.10, f32[2048]{0:T(1024)S(1)} %get-tuple-element.9), kind=kOutput, calls=%fused_computation.13 | convolution fusion | flops 5644713984 | bytes 30547968 | tf_op jit(solution)/shard_map/dot_general | solution.py:37
  292.8 0.0 all-reduce.4.cloned.1.call-update
  292.9 101.6 %reduce-scatter.2.cloned.1.call-done = f32[256,3584]{1,0:T(8,128)} async-done(((f32[1024,3584]{1,0:T(8,128)}), f32[256,3584]{1,0:T(8,128)}) %reduce-scatter.2.cloned.1.call-update) | async-done | bytes 3670032 | tf_op jit(solution)/shard_map/reduce_scatter | solution.py:22
  394.5 3.4 convert_element_type.21
  397.9 53.5 %all-reduce.6.cloned.1.call-done = f32[2048,64]{0,1:T(8,128)} async-done(((f32[2048,64]{0,1:T(8,128)}), f32[2048,64]{0,1:T(8,128)}) %all-reduce.6.cloned.1.call-update) | async-done | bytes 524304 | tf_op jit(solution)/shard_map/psum | solution.py:49
  451.4 55.4 %all-reduce.4.cloned.1.call-done = f32[64,3584]{1,0:T(8,128)} async-done(((f32[64,3584]{1,0:T(8,128)}), f32[64,3584]{1,0:T(8,128)}) %all-reduce.4.cloned.1.call-update) | async-done | bytes 917520 | tf_op jit(solution)/shard_map/psum | solution.py:43
  506.8 2.2 copy.14
  509.0 1.9 copy.15
Async XLA Ops:
  7.2 53.9 %copy-start = (bf16[64,3584]{1,0:T(8,128)(2,1)S(1)}, bf16[64,3584]{1,0:T(8,128)(2,1)}, u32[]{:S(2)}) copy-start(bf16[64,3584]{1,0:T(8,128)(2,1)} %param.9) | copy-start | bytes 1376260
  7.2 49.0 %all-gather.3.cloned.1.call-start = ((), (), s32[]{:S(2)}) async-start(), calls=%async_computation.2 | async-start | bytes 4718592 | tf_op jit(solution)/shard_map/all_gather | solution.py:11
  9.3 166.6 %all-gather.5.cloned.1.call-start = ((), (), s32[]{:S(2)}) async-start(), calls=%async_computation.4 | async-start | bytes 9175040 | tf_op jit(solution)/shard_map/all_gather | solution.py:31
  56.2 72.6 %all-to-all-start = ((bf16[256,4,2048]{0,2,1:T(8,128)(2,1)}), bf16[256,4,2048]{0,2,1:T(8,128)(2,1)}, u32[]{:S(2)}, u32[]{:S(2)}) async-start(bf16[256,4,2048]{0,2,1:T(8,128)(2,1)} %bitcast.11), calls=%async_computation | async-start | bytes 8388608 | tf_op jit(solution)/shard_map/all_to_all | solution.py:12
  61.0 333.4 %reduce-scatter.2.cloned.1.call-start = ((), (), s32[]{:S(2)}) async-start(), calls=%async_computation.3 | async-start | bytes 18350080 | tf_op jit(solution)/shard_map/reduce_scatter | solution.py:22
  175.9 52.5 %copy-start.2 = (f32[2048]{0:T(1024)S(1)}, f32[2048]{0:T(1024)}, u32[]{:S(2)}) copy-start(f32[2048]{0:T(1024)} %param.11) | copy-start | bytes 24580
  253.8 197.6 %all-reduce.6.cloned.1.call-start = ((), (), s32[]{:S(2)}) async-start(), calls=%async_computation.6 | async-start | bytes 1048576 | tf_op jit(solution)/shard_map/psum | solution.py:49
  253.8 21.3 %copy-start.1 = (bf16[2048,64]{0,1:T(8,128)(2,1)S(1)}, bf16[2048,64]{0,1:T(8,128)(2,1)}, u32[]{:S(2)}) copy-start(bf16[2048,64]{0,1:T(8,128)(2,1)} %param.10) | copy-start | bytes 786436
  274.9 231.9 %all-reduce.4.cloned.1.call-start = ((), (), s32[]{:S(2)}) async-start(), calls=%async_computation.5 | async-start | bytes 1835008 | tf_op jit(solution)/shard_map/psum | solution.py:43
Sparse Core Ops, SparseCore 0:
  10.2 45.9 all-gather.2
  58.0 117.8 all-gather.4
  253.9 140.4 reduce-scatter.1
  397.2 54.1 all-reduce.5
  455.2 51.5 all-reduce.3
where the time goes:
time: 520 us; the launch traced here: 517 us
  waiting for transfers between devices  350 us (67%)
  matrix products  109 us (21%)
  blocking collectives  23.2 us (4%)
  between operations  13.8 us (3%)
  local copies, waits for them, and re-layouts  12.4 us (2%)
  starting transfers between devices  5.26 us (1%)
    reduce_scatter x1, waiting for transfers between devices, local(): lax.psum_scatter(jnp.dot(scaled_rows, merged_b, preferred_element_type=jn...  102 us
    psum x1, waiting for transfers between devices, local(): adapter_down_gradient = lax.psum(down_partial_sum, 'dp')  55.4 us
    psum x1, waiting for transfers between devices, local(): adapter_up_gradient = lax.psum(up_partial_sum, 'tensor')  53.5 us
    all_to_all x1, waiting for transfers between devices, local(): lax.all_to_all(full_grad, 'dp', split_axis=1, concat_axis=0, tiled=True)  51.9 us
    all_gather x1, waiting for transfers between devices, local(): full_grad = lax.all_gather(output_gradient, 'tensor', axis=1, tiled=True)  46.1 us
    all_gather x1, waiting for transfers between devices, local(): lax.all_gather(inputs, 'dp', axis=0, tiled=True)  40.8 us
    dot_general x1, matrix products, local(): lax.dot_general(row_grad, lax.all_gather(inputs, 'dp', axis=0, tiled=True...  29.3 us
    dot_general x1, matrix products, local(): jnp.dot(scaled_rows, merged_b, preferred_element_type=jnp.float32)  24.8 us
  transfers between devices with their start and end apart: 6, of which 6 were waited for; matrix products, arithmetic and copies ran while one was open for 12% of the time, Pallas kernels for 0%

commit v1 on v0

v1 whole, which is shorter than its diff:
```python
import jax
import jax.numpy as jnp
from jax import lax
from jax.sharding import PartitionSpec as P

adapter_scale = 2.0
epsilon = 1e-06
bf16, f32 = jnp.bfloat16, jnp.float32


def two_parts(value):
    high = value.astype(bf16)
    return high, (value - high.astype(f32)).astype(bf16)


def mm(a, b, ca, cb):
    return lax.dot_general(a, b, (((ca,), (cb,)), ((), ())), preferred_element_type=f32)


def local(inputs, output_gradient, frozen, down, up, magnitude):
    nd, nt = lax.axis_size("dp"), lax.axis_size("tensor")
    k = nt // nd
    tokens, columns = inputs.shape
    rank = down.shape[0]
    me = lax.axis_index("dp")
    same = [[m + k * q for q in range(nd)] for m in range(k)]
    near = [[k * q + m for m in range(k)] for q in range(nd)]
    part = lax.all_gather(output_gradient, "tensor", axis=0, axis_index_groups=same)
    part = lax.all_to_all(part, "dp", split_axis=0, concat_axis=0)
    grad = lax.all_gather(part, "tensor", axis=2, axis_index_groups=near, tiled=True)
    grad = grad.reshape(nd * tokens, -1)
    x_down = lax.psum(mm(inputs, down, 1, 1), "tensor")
    x_down = lax.all_gather(x_down, "dp", axis=0, tiled=True)
    all_inputs = lax.all_gather(inputs, "dp", axis=0, tiled=True)

    merged = frozen.astype(f32) + adapter_scale * mm(up, down, 1, 0)
    merged_b = merged.astype(bf16)
    squares = lax.psum(jnp.sum(merged * merged, axis=1), "tensor")
    norm = jnp.sqrt(squares + epsilon)
    scale = magnitude / norm
    scaled = (grad.astype(f32) * scale[None, :]).astype(bf16)

    blocks = [((me ^ s) * tokens) for s in range(nd)]

    def share(start):
        return mm(lax.dynamic_slice_in_dim(scaled, start, tokens, 0), merged_b, 1, 0)

    def swap(value, s):
        return lax.ppermute(value, "dp", [(i, i ^ s) for i in range(nd)])

    half = tokens // 2
    far = share(blocks[3]).astype(bf16)
    on_1 = share(blocks[1])
    on_2 = share(blocks[2])
    a1, b1 = swap(far[:half], 1), swap(far[half:], 2)
    a2, b2 = swap(on_1[:half].astype(bf16), 1), swap(on_2[half:].astype(bf16), 2)
    own = share(blocks[0])
    a3 = swap((on_2[:half] + a1.astype(f32)).astype(bf16), 2)
    b3 = swap((on_1[half:] + b1.astype(f32)).astype(bf16), 1)
    first = own[:half] + a2.astype(f32) + a3.astype(f32)
    second = own[half:] + b2.astype(f32) + b3.astype(f32)
    input_gradient_rows = jnp.concatenate([first, second], 0).astype(bf16)

    high, low = two_parts(scale[:, None] * up.astype(f32))
    both = mm(grad, jnp.concatenate([high, low], 1), 1, 0)
    g_up = lax.psum(both[:, :rank] + both[:, rank:], "dp")
    high, low = two_parts(g_up)
    both = mm(jnp.concatenate([high, low], 1), all_inputs, 0, 0)
    adapter_down_gradient = adapter_scale * (both[:rank] + both[rank:])
    high, low = two_parts(x_down)
    both = mm(grad, jnp.concatenate([high, low], 1), 0, 0)
    product_down = both[:, :rank] + both[:, rank:]
    adapter_up_gradient = adapter_scale * scale[:, None] * product_down
    y = mm(all_inputs, frozen, 1, 1)
    sums = lax.psum(jnp.sum(y * grad.astype(f32), axis=0), "tensor")
    sums = sums + adapter_scale * jnp.sum(up.astype(f32) * product_down, axis=1)
    return input_gradient_rows, adapter_down_gradient, adapter_up_gradient, sums / norm


def solution(mesh):
    placed = (
        P("dp", "tensor"),
        P("dp", "tensor"),
        P("dp", "tensor"),
        P(None, "tensor"),
        P("dp", None),
        P("dp"),
    )
    return jax.shard_map(
        local,
        mesh=mesh,
        in_specs=placed,
        out_specs=(P("dp", "tensor"), P(None, "tensor"), P("dp", None), P("dp")),
        check_vma=False,
    )
```

time: 520 us -> 325 us (0.62)
  waiting for transfers between devices: 350 us -> 173 us
  matrix products: 109 us -> 70.4 us
  blocking collectives: 23.2 us -> 34.7 us
  other arithmetic: 4.06 us -> 13 us
  local copies, waits for them, and re-layouts: 12.4 us -> 5.54 us
    reduce_scatter x1 -> x0, waiting for transfers between devices: 102 us -> none  [local(): lax.psum_scatter(jnp.dot(scaled_rows, merged_b, preferred_element_type=jn...]
    psum x2, waiting for transfers between devices: 109 us -> 28.2 us  [the longest x1 17.6 us: local(): x_down = lax.psum(mm(inputs, down, 1, 1), 'tensor')]
    dot_general x5 -> x10, matrix products: 109 us -> 70.4 us  [mm(): lax.dot_general(a, b, (((ca,), (cb,)), ((), ())), preferred_element_type=...]
    all_to_all x1, waiting for transfers between devices: 51.9 us -> 22.4 us  [local(): part = lax.all_to_all(part, 'dp', split_axis=0, concat_axis=0)]
    ppermute x0 -> x6, waiting for transfers between devices: none -> 22.1 us  [swap(): return lax.ppermute(value, 'dp', [(i, i ^ s) for i in range(nd)])]
    all_gather x2 -> x3, waiting for transfers between devices: 86.9 us -> 98.8 us  [the longest x1 52.4 us: local(): all_inputs = lax.all_gather(inputs, 'dp', axis=0, tiled=True)]
    all_gather x0 -> x1, blocking collectives: none -> 11.5 us  [local(): x_down = lax.all_gather(x_down, 'dp', axis=0, tiled=True)]
    all_to_all x1 -> x0, local copies, waits for them, and re-layouts: 6.29 us -> none  [local(): lax.all_to_all(full_grad, 'dp', split_axis=1, concat_axis=0, tiled=True)]
  transfers between devices with their start and end apart: 6 -> 12, of which waited for: 6 -> 7; matrix products, arithmetic and copies ran while one was open for 12% -> 18% of each run, Pallas kernels for 0% -> 0%
where the time goes in v1:
time: 325 us; the launch traced here: 322 us
  waiting for transfers between devices  173 us (53%)
  matrix products  70.4 us (22%)
  blocking collectives  34.7 us (11%)
  between operations  15.5 us (5%)
  other arithmetic  13 us (4%)
  starting transfers between devices  10 us (3%)
  local copies, waits for them, and re-layouts  5.54 us (2%)
    dot_general x10, matrix products, mm(): lax.dot_general(a, b, (((ca,), (cb,)), ((), ())), preferred_element_type=...  70.4 us
    all_gather x1, waiting for transfers between devices, local(): all_inputs = lax.all_gather(inputs, 'dp', axis=0, tiled=True)  52.4 us
    all_gather x1, waiting for transfers between devices, local(): lax.all_gather(output_gradient, 'tensor', axis=0, axis_index_groups=same)  46.4 us
    psum x1, blocking collectives, local(): squares = lax.psum(jnp.sum(merged * merged, axis=1), 'tensor')  23.2 us
    all_to_all x1, waiting for transfers between devices, local(): part = lax.all_to_all(part, 'dp', split_axis=0, concat_axis=0)  22.4 us
    ppermute x6, waiting for transfers between devices, swap(): return lax.ppermute(value, 'dp', [(i, i ^ s) for i in range(nd)])  22.1 us
    psum x1, waiting for transfers between devices, local(): x_down = lax.psum(mm(inputs, down, 1, 1), 'tensor')  17.6 us
    all_gather x1, blocking collectives, local(): x_down = lax.all_gather(x_down, 'dp', axis=0, tiled=True)  11.5 us
  transfers between devices with their start and end apart: 12, of which 7 were waited for; matrix products, arithmetic and copies ran while one was open for 18% of the time, Pallas kernels for 0%

profile of v1, /device:TPU:24, one launch (start us, length us, event | category | flops | bytes accessed | tf_op | source)
XLA Modules:
  0.0 322.1 jit_solution(4288192721623825283)
XLA Ops:
  8.0 0.0 copy-start
  8.0 0.0 all-gather.9.cloned.1.call-start
  8.1 0.7 all-gather.9.cloned.1.call-update
  8.7 46.4 %all-gather.9.cloned.1.call-done = bf16[1024,1024]{1,0:T(8,128)(2,1)} async-done(((bf16[256,1024]{1,0:T(8,128)(2,1)}), bf16[1024,1024]{1,0:T(8,128)(2,1)}) %all-gather.9.cloned.1.call-update) | async-done | bytes 2097168 | tf_op jit(solution)/shard_map/all_gather | solution.py:28
  55.2 3.6 %all-to-all-start = ((bf16[4,256,1024]{2,1,0:T(8,128)(2,1)}), bf16[4,256,1024]{2,1,0:T(8,128)(2,1)S(1)}, u32[]{:S(2)}, u32[]{:S(2)}) async-start(bf16[4,256,1024]{2,1,0:T(8,128)(2,1)} %bitcast.23), calls=%async_computation | async-start | bytes 4194304 | tf_op jit(solution)/shard_map/all_to_all | solution.py:29
  58.8 0.0 all-reduce.6.cloned.1.call-start
  58.9 2.8 fusion.41
  61.7 0.0 all-reduce.6.cloned.1.call-update
  61.7 0.0 all-gather.5.cloned.1.call-start
  61.8 22.4 %all-to-all-done = bf16[4,256,1024]{2,1,0:T(8,128)(2,1)S(1)} async-done(((bf16[4,256,1024]{2,1,0:T(8,128)(2,1)}), bf16[4,256,1024]{2,1,0:T(8,128)(2,1)S(1)}, u32[]{:S(2)}, u32[]{:S(2)}) %all-to-all-start) | async-done | bytes 2097184 | tf_op jit(solution)/shard_map/all_to_all | solution.py:29
  84.1 1.3 copy-done.2
  85.4 0.0 all-gather.5.cloned.1.call-update
  85.5 0.0 all-gather.7.cloned.1.call-start
  85.5 0.7 all-gather.7.cloned.1.call-update
  86.2 0.0 all-reduce.4.cloned.1.call-start
  86.3 12.6 %multiply_reduce_fusion = (f32[2048]{0:T(1024)S(1)}, bf16[2048,3584]{1,0:T(8,128)(2,1)}) fusion(bf16[2048,3584]{1,0:T(8,128)(2,1)} %param.8, bf16[2048,64]{0,1:T(8,128)(2,1)S(1)} %copy-done.8, bf16[64,3584]{1,0:T(8,128)(2,1)S(1)} %copy-done), kind=kOutput, calls=%fused_computation | convolution fusion | flops 983562240 | bytes 30089216 | tf_op jit(solution)/shard_map/dot_general | solution.py:17
  98.8 17.6 %all-reduce.6.cloned.1.call-done = f32[256,64]{0,1:T(8,128)} async-done(((f32[256,64]{0,1:T(8,128)}), f32[256,64]{0,1:T(8,128)}) %all-reduce.6.cloned.1.call-update) | async-done | bytes 65552 | tf_op jit(solution)/shard_map/psum | solution.py:32
  116.5 11.5 %all_gather.19 = f32[1024,64]{0,1:T(8,128)S(1)} all-gather(f32[256,64]{0,1:T(8,128)} %all-reduce.6.cloned.1.call-done), channel_id=1, replica_groups=mesh['dp'=4,'tensor'=8] {'dp'}, dimensions={0}, use_global_device_ids=true | all-gather | bytes 327680 | tf_op jit(solution)/shard_map/all_gather | solution.py:33
  128.0 0.0 all-gather.5.cloned.1.call-done
  128.0 2.9 convolution_bitcast_fusion
  130.9 0.0 copy-start.9
  131.0 52.4 %all-gather.7.cloned.1.call-done = bf16[1024,3584]{1,0:T(8,128)(2,1)} async-done(((bf16[256,3584]{1,0:T(8,128)(2,1)}), bf16[1024,3584]{1,0:T(8,128)(2,1)}) %all-gather.7.cloned.1.call-update) | async-done | bytes 7340048 | tf_op jit(solution)/shard_map/all_gather | solution.py:34
  183.3 20.6 %fusion.2 = f32[2048]{0:T(1024)S(1)} fusion(bf16[1024,2048]{1,0:T(8,128)(2,1)} %bitcast.21, bf16[1024,3584]{1,0:T(8,128)(2,1)} %all-gather.7.cloned.1.call-done, bf16[2048,3584]{1,0:T(8,128)(2,1)} %param.8), kind=kOutput, calls=%fused_computation.6 | convolution fusion | flops 15038674944 | bytes 26222592 | tf_op jit(solution)/shard_map/dot_general | solution.py:17
  203.9 23.2 %all-reduce = (f32[2048]{0:T(1024)S(1)}, f32[2048]{0:T(1024)S(1)}) all-reduce(f32[2048]{0:T(1024)S(1)} %get-tuple-element.12, f32[2048]{0:T(1024)S(1)} %fusion.2), channel_id=1, replica_groups=mesh['dp'=4,'tensor'=8] {'tensor'}, use_global_device_ids=true, to_apply=%region_1.0 | all-reduce | flops 4096 | bytes 32768 | tf_op jit(solution)/shard_map/psum | solution.py:38
  227.1 0.9 fusion.20
  228.1 3.7 %convolution_bitcast_fusion.1 = f32[1024,128]{0,1:T(8,128)S(1)} fusion(bf16[1024,2048]{1,0:T(8,128)(2,1)} %bitcast.22, bf16[2048,64]{0,1:T(8,128)(2,1)S(1)} %get-tuple-element.22, bf16[2048,64]{0,1:T(8,128)(2,1)S(1)} %get-tuple-element.23), kind=kOutput, calls=%fused_computation.22 | convolution fusion | flops 537919488 | bytes 5242880 | tf_op jit(solution)/shard_map/dot_general | solution.py:17
  231.8 0.7 slice_add_fusion.6
  232.5 0.0 all-reduce.4.cloned.1.call-update
  232.5 0.0 slice-start
  232.5 3.6 %fusion.1 = bf16[1024,2048]{1,0:T(8,128)(2,1)S(1)} fusion(f32[2048]{0:T(1024)S(1)} %get-tuple-element.9, bf16[4,256,2048]{2,1,0:T(8,128)(2,1)} %all-gather.5.cloned.1.call-done), kind=kLoop, calls=%fused_computation.5 | loop fusion | flops 6291456 | bytes 8396800 | tf_op jit(solution)/shard_map/convert_element_type | solution.py:41
  236.1 0.0 slice-start.1
  236.1 0.0 slice-start.2
  236.1 0.0 slice-start.3
  236.2 9.4 %convolution_convert_fusion = bf16[256,3584]{1,0:T(8,128)(2,1)S(1)} fusion(bf16[2048,3584]{1,0:T(8,128)(2,1)} %get-tuple-element.13, bf16[1024,2048]{1,0:T(8,128)(2,1)S(1)} %fusion.1, s32[]{:T(128)S(6)} %select_n.15), kind=kOutput, calls=%fused_computation.7 | convolution fusion | flops 3759013888 | bytes 17563652 | tf_op jit(solution)/shard_map/dot_general | solution.py:17
  245.5 1.0 fusion.40
  246.6 1.5 collective-permute-start.1
  248.1 0.5 collective-permute-start.4
  248.5 0.0 slice-done.2
  248.6 4.0 %fusion.10 = f32[256,3584]{1,0:T(8,128)S(1)} fusion(bf16[2048,3584]{1,0:T(8,128)(2,1)S(1)} %bitcast.25, bf16[1024,2048]{1,0:T(8,128)(2,1)S(1)} %fusion.1, s32[]{:T(128)S(6)} %select_n.14), kind=kOutput, calls=%fused_computation.24 | convolution fusion | flops 3758096384 | bytes 19398660 | tf_op jit(solution)/shard_map/dot_general | solution.py:17
  252.6 1.1 slice.106
  253.7 1.0 copy-done.6
  254.7 1.5 collective-permute-start.3
  256.3 4.0 %fusion.12 = f32[256,3584]{1,0:T(8,128)S(1)} fusion(bf16[2048,3584]{1,0:T(8,128)(2,1)S(1)} %bitcast.25, bf16[1024,2048]{1,0:T(8,128)(2,1)S(1)} %fusion.1, s32[]{:T(128)S(6)} %select_n.13), kind=kOutput, calls=%fused_computation.26 | convolution fusion | flops 3758096384 | bytes 19398660 | tf_op jit(solution)/shard_map/dot_general | solution.py:17
  260.3 6.0 %fusion.14 = f32[256,3584]{1,0:T(8,128)} fusion(bf16[2048,3584]{1,0:T(8,128)(2,1)S(1)} %bitcast.25, bf16[1024,2048]{1,0:T(8,128)(2,1)S(1)} %fusion.1, s32[]{:T(128)S(6)} %select_n.12), kind=kOutput, calls=%fused_computation.28 | convolution fusion | flops 3758096384 | bytes 19398660 | tf_op jit(solution)/shard_map/dot_general | solution.py:17
  266.3 0.0 copy-done.4
  266.3 1.0 slice.107
  267.3 0.6 collective-permute-start
  267.9 0.6 add_divide_fusion
  268.5 10.6 %all-reduce.4.cloned.1.call-done = f32[1024,64]{0,1:T(8,128)} async-done(((f32[1024,64]{0,1:T(8,128)}), f32[1024,64]{0,1:T(8,128)}) %all-reduce.4.cloned.1.call-update) | async-done | bytes 262160 | tf_op jit(solution)/shard_map/psum | solution.py:66
  279.1 1.1 subtract_convert_fusion.1
  280.2 4.4 %fusion.24 = f32[128,3584]{1,0:T(8,128)S(1)} fusion(bf16[1024,3584]{1,0:T(8,128)(2,1)} %all-gather.7.cloned.1.call-done, bf16[1024,64]{0,1:T(8,128)(2,1)S(1)} %get-tuple-element.10, bf16[1024,64]{0,1:T(8,128)(2,1)S(1)} %get-tuple-element.11), kind=kOutput, calls=%fused_computation.43 | convolution fusion | flops 940048384 | bytes 9437184 | tf_op jit(solution)/shard_map/dot_general | solution.py:17
  284.6 0.0 collective-permute-done.1
  284.6 1.6 fusion.6
  286.1 1.4 collective-permute-start.2
  287.6 0.0 collective-permute-done.4
  287.6 1.4 fusion.3
  289.0 0.7 collective-permute-start.5
  289.7 1.0 fusion.16
  290.7 2.5 collective-permute-done.3
  293.2 0.0 collective-permute-done
  293.2 19.7 %collective-permute-done.2 = bf16[128,3584]{1,0:T(8,128)(2,1)S(1)} collective-permute-done((bf16[128,3584]{1,0:T(8,128)(2,1)S(1)}, bf16[128,3584]{1,0:T(8,128)(2,1)S(1)}, u32[]{:S(2)}, u32[]{:S(2)}) %collective-permute-start.2) | collective-permute-done | bytes 917536 | tf_op jit(solution)/shard_map/ppermute | solution.py:49
  312.8 0.0 collective-permute-done.5
  312.8 0.7 fusion.8
  313.6 1.3 pad_maximum_fusion
  (21 shorter events, 0.1 us)
Async XLA Ops:
  8.0 50.9 %copy-start = (bf16[64,3584]{1,0:T(8,128)(2,1)S(1)}, bf16[64,3584]{1,0:T(8,128)(2,1)}, u32[]{:S(2)}) copy-start(bf16[64,3584]{1,0:T(8,128)(2,1)} %param.9) | copy-start | bytes 1376260
  8.0 47.2 %all-gather.9.cloned.1.call-start = ((), (), s32[]{:S(2)}) async-start(), calls=%async_computation.5 | async-start | bytes 2621440 | tf_op jit(solution)/shard_map/all_gather | solution.py:28
  55.2 28.9 %all-to-all-start = ((bf16[4,256,1024]{2,1,0:T(8,128)(2,1)}), bf16[4,256,1024]{2,1,0:T(8,128)(2,1)S(1)}, u32[]{:S(2)}, u32[]{:S(2)}) async-start(bf16[4,256,1024]{2,1,0:T(8,128)(2,1)} %bitcast.23), calls=%async_computation | async-start | bytes 4194304 | tf_op jit(solution)/shard_map/all_to_all | solution.py:29
  58.8 27.4 %copy-start.8 = (bf16[2048,64]{0,1:T(8,128)(2,1)S(1)}, bf16[2048,64]{0,1:T(8,128)(2,1)}, u32[]{:S(2)}) copy-start(bf16[2048,64]{0,1:T(8,128)(2,1)} %param.10) | copy-start | bytes 786436
  58.8 57.6 %all-reduce.6.cloned.1.call-start = ((), (), s32[]{:S(2)}) async-start(), calls=%async_computation.4 | async-start | bytes 131072 | tf_op jit(solution)/shard_map/psum | solution.py:32
  61.7 66.3 %all-gather.5.cloned.1.call-start = ((), (), s32[]{:S(2)}) async-start(), calls=%async_computation.1 | async-start | bytes 6291456 | tf_op jit(solution)/shard_map/all_gather | solution.py:30
  84.1 1.3 copy-start.2
  85.5 97.9 %all-gather.7.cloned.1.call-start = ((), (), s32[]{:S(2)}) async-start(), calls=%async_computation.3 | async-start | bytes 9175040 | tf_op jit(solution)/shard_map/all_gather | solution.py:34
  86.2 192.9 %all-reduce.4.cloned.1.call-start = ((), (), s32[]{:S(2)}) async-start(), calls=%async_computation.2 | async-start | bytes 524288 | tf_op jit(solution)/shard_map/psum | solution.py:66
  130.9 96.2 %copy-start.9 = (f32[2048]{0:T(1024)S(1)}, f32[2048]{0:T(1024)}, u32[]{:S(2)}) copy-start(f32[2048]{0:T(1024)} %param.11) | copy-start | bytes 24580
  232.5 16.0 %slice-start = ((s8[14680064]{0:T(1024)(128)(4,1)}), s8[4194304]{0:T(1024)(128)(4,1)S(1)}, s32[]{:S(2)}) async-start(s8[14680064]{0:T(1024)(128)(4,1)} %bitcast.24), calls=%async_computation.6 | async-start | bytes 8388608
  236.1 12.4 %slice-start.1 = ((s8[14680064]{0:T(1024)(128)(4,1)}), s8[4194304]{0:T(1024)(128)(4,1)S(1)}, s32[]{:S(2)}) async-start(s8[14680064]{0:T(1024)(128)(4,1)} %bitcast.24), calls=%async_computation.7 | async-start | bytes 8388608
  236.1 12.4 %slice-start.2 = ((s8[14680064]{0:T(1024)(128)(4,1)}), s8[4194304]{0:T(1024)(128)(4,1)S(1)}, s32[]{:S(2)}) async-start(s8[14680064]{0:T(1024)(128)(4,1)} %bitcast.24), calls=%async_computation.8 | async-start | bytes 8388608
  236.1 12.4 %slice-start.3 = ((s8[14680064]{0:T(1024)(128)(4,1)}), s8[2097152]{0:T(1024)(128)(4,1)S(1)}, s32[]{:S(2)}) async-start(s8[14680064]{0:T(1024)(128)(4,1)} %bitcast.24), calls=%async_computation.9 | async-start | bytes 4194304
  246.6 38.0 %collective-permute-start.1 = (bf16[128,3584]{1,0:T(8,128)(2,1)}, bf16[128,3584]{1,0:T(8,128)(2,1)}, u32[]{:S(2)}, u32[]{:S(2)}) collective-permute-start(bf16[128,3584]{1,0:T(8,128)(2,1)} %get-tuple-element.16), channel_id=1, source_target_pairs={{0,8},{8,0},{16,24},{24,16},{1,9},{9,1},{17,25},{25,17},{2,10},{10... | collective-permute-start | bytes 2752520 | tf_op jit(solution)/shard_map/ppermute | solution.py:49
  248.1 39.5 %collective-permute-start.4 = (bf16[128,3584]{1,0:T(8,128)(2,1)S(1)}, bf16[128,3584]{1,0:T(8,128)(2,1)}, u32[]{:S(2)}, u32[]{:S(2)}) collective-permute-start(bf16[128,3584]{1,0:T(8,128)(2,1)S(1)} %get-tuple-element.17), channel_id=1, source_target_pairs={{0,16},{8,24},{16,0},{24,8},{1,17},{9,25},{17,1},{25,9},{2,18},{10... | collective-permute-start | bytes 2752520 | tf_op jit(solution)/shard_map/ppermute | solution.py:49
  252.6 2.1 copy-start.6
  254.7 38.4 %collective-permute-start.3 = (bf16[128,3584]{1,0:T(8,128)(2,1)}, bf16[128,3584]{1,0:T(8,128)(2,1)S(1)}, u32[]{:S(2)}, u32[]{:S(2)}) collective-permute-start(bf16[128,3584]{1,0:T(8,128)(2,1)} %slice.106), channel_id=1, source_target_pairs={{0,16},{8,24},{16,0},{24,8},{1,17},{9,25},{17,1},{25,9},{2,18},{10... | collective-permute-start | bytes 2752520 | tf_op jit(solution)/shard_map/ppermute | solution.py:49
  260.3 6.0 %copy-start.4 = (f32[256,3584]{1,0:T(8,128)}, f32[256,3584]{1,0:T(8,128)S(1)}, u32[]{:S(2)}) copy-start(f32[256,3584]{1,0:T(8,128)S(1)} %fusion.12) | copy-start | bytes 11010052
  267.3 25.8 %collective-permute-start = (bf16[128,3584]{1,0:T(8,128)(2,1)}, bf16[128,3584]{1,0:T(8,128)(2,1)S(1)}, u32[]{:S(2)}, u32[]{:S(2)}) collective-permute-start(bf16[128,3584]{1,0:T(8,128)(2,1)} %slice.107), channel_id=1, source_target_pairs={{0,8},{8,0},{16,24},{24,16},{1,9},{9,1},{17,25},{25,17},{2,10},{10... | collective-permute-start | bytes 2752520 | tf_op jit(solution)/shard_map/ppermute | solution.py:49
  280.2 4.4 %copy-start.7 = (f32[256,3584]{1,0:T(8,128)S(1)}, f32[256,3584]{1,0:T(8,128)}, u32[]{:S(2)}) copy-start(f32[256,3584]{1,0:T(8,128)} %copy-done.6) | copy-start | bytes 11010052
  280.2 7.4 %copy-start.5 = (f32[256,3584]{1,0:T(8,128)S(1)}, f32[256,3584]{1,0:T(8,128)}, u32[]{:S(2)}) copy-start(f32[256,3584]{1,0:T(8,128)} %copy-done.4) | copy-start | bytes 11010052
  284.6 28.3 %copy-start.3 = (f32[256,3584]{1,0:T(8,128)S(1)}, f32[256,3584]{1,0:T(8,128)}, u32[]{:S(2)}) copy-start(f32[256,3584]{1,0:T(8,128)} %fusion.14) | copy-start | bytes 11010052
  286.1 26.7 %collective-permute-start.2 = (bf16[128,3584]{1,0:T(8,128)(2,1)S(1)}, bf16[128,3584]{1,0:T(8,128)(2,1)S(1)}, u32[]{:S(2)}, u32[]{:S(2)}) collective-permute-start(bf16[128,3584]{1,0:T(8,128)(2,1)S(1)} %fusion.6), channel_id=1, source_target_pairs={{0,16},{8,24},{16,0},{24,8},{1,17},{9,25},{17,1},{25,9},{2,18},{10... | collective-permute-start | bytes 2752520 | tf_op jit(solution)/shard_map/ppermute | solution.py:49
  289.0 23.9 %collective-permute-start.5 = (bf16[128,3584]{1,0:T(8,128)(2,1)S(1)}, bf16[128,3584]{1,0:T(8,128)(2,1)S(1)}, u32[]{:S(2)}, u32[]{:S(2)}) collective-permute-start(bf16[128,3584]{1,0:T(8,128)(2,1)S(1)} %fusion.3), channel_id=1, source_target_pairs={{0,8},{8,0},{16,24},{24,16},{1,9},{9,1},{17,25},{25,17},{2,10},{10... | collective-permute-start | bytes 2752520 | tf_op jit(solution)/shard_map/ppermute | solution.py:49
  289.7 25.2 %copy-start.1 = (bf16[64,3584]{1,0:T(8,128)(2,1)S(1)}, bf16[64,3584]{1,0:T(8,128)(2,1)}, u32[]{:S(2)}) copy-start(bf16[64,3584]{1,0:T(8,128)(2,1)} %param.9) | copy-start | bytes 1376260
Sparse Core Ops, SparseCore 0:
  10.4 44.7 all-gather.8
  85.6 13.9 all-gather.4
  101.4 81.8 all-gather.6
  232.6 46.4 all-reduce.3
Sparse Core Ops, SparseCore 1:
  62.2 54.2 all-reduce.5

commit v2 on v1

v2 whole, which is shorter than its diff:
```python
import functools

import jax
import jax.numpy as jnp
from jax import lax
from jax.experimental import pallas as pl
from jax.experimental.pallas import tpu as pltpu
from jax.sharding import PartitionSpec as P

adapter_scale = 2.0
epsilon = 1e-06
bf16, f32 = jnp.bfloat16, jnp.float32
MESH = pl.DeviceIdType.MESH


def mm(a, b, ca, cb):
    return lax.dot_general(a, b, (((ca,), (cb,)), ((), ())), preferred_element_type=f32)


def kernel(
    nd, nt, n_local,
    x_ref, g_ref, w_ref, down_ref, up_ref, upt_ref, mag_ref,
    dx_ref, dg_ref, ug_ref, mg_ref,
    w, x, gz, grad, scaled, part, own, got, u_part, u, v, squares, sums,
    send, recv, local_sem,
):
    d, t = lax.axis_index("dp"), lax.axis_index("tensor")
    k = nt // nd
    q, m = t // k, t % k
    tokens, columns = x_ref.shape
    rows = w_ref.shape[0]
    nr = g_ref.shape[1]
    half = tokens // 2
    n_tile = 7
    width = columns // n_tile
    side = 256
    p1, p2, p3 = d + 1 - 2 * (d % 2), (d + 2) % nd, nd - 1 - d
    started, used = [], [0]

    def remote(src, dst, to):
        i = used[0]
        used[0] += 1
        copy = pltpu.make_async_remote_copy(
            src_ref=src, dst_ref=dst, send_sem=send.at[i], recv_sem=recv.at[i],
            device_id=to, device_id_type=MESH,
        )
        started.append(copy)
        copy.start()
        return copy

    def block(index, size=None, offset=0):
        return pl.ds(pl.multiple_of(index * tokens + offset, half), size or tokens)

    load_x = pltpu.make_async_copy(x_ref, x.at[block(d)], local_sem.at[0])
    load_x.start()
    load_g = pltpu.make_async_copy(g_ref, gz.at[q], local_sem.at[1])
    load_g.start()
    load_w = pltpu.make_async_copy(w_ref, w, local_sem.at[2])
    load_w.start()

    barrier = pltpu.get_barrier_semaphore()
    for peer in (p1, p2, p3):
        pl.semaphore_signal(barrier, inc=1, device_id=(peer, t), device_id_type=MESH)
    for o in range(1, nt):
        pl.semaphore_signal(barrier, inc=1, device_id=(d, (t + o) % nt), device_id_type=MESH)
    pl.semaphore_wait(barrier, nd - 1 + nt - 1)

    def share_out(slots):
        return [remote(slots.at[t], slots.at[t], (d, (t + o) % nt)) for o in range(1, nt)]

    x1 = remote(x_ref, x.at[block(d)], (p1, t))
    x2 = remote(x_ref, x.at[block(d)], (p2, t))
    gathered = [
        remote(g_ref, gz.at[q], (d, ((q + o) % nd) * k + m)) for o in range(1, nd)
    ]

    load_x.wait()
    u_part[t] = mm(down_ref[...], x[block(d)], 1, 1)
    u_sent = share_out(u_part)

    load_w.wait()

    @pl.loop(0, rows // side)
    def _(i):
        r = pl.ds(pl.multiple_of(i * side, side), side)
        total = jnp.zeros((side, 128), f32)
        for c in range(n_tile):
            cols = slice(c * width, (c + 1) * width)
            merged = w[r, cols].astype(f32) + adapter_scale * mm(up_ref[r, :], down_ref[:, cols], 1, 0)
            w[r, cols] = merged.astype(bf16)
            square = merged * merged
            for lane in range(0, width, 128):
                total = total + square[:, lane:lane + 128]
        squares[t, :, r] = jnp.sum(total.T, axis=0, keepdims=True)

    squares_sent = share_out(squares)

    load_g.wait()
    for copy in gathered:
        copy.wait_recv()
    moved = [
        remote(gz.at[p], grad.at[m, block(d)], (p, t)) for p in (p3, p1, p2)
    ]
    keep_g = pltpu.make_async_copy(gz.at[d], grad.at[m, block(d)], local_sem.at[3])
    keep_g.start()

    def near(source):
        return [
            remote(grad.at[m, block(source)], grad.at[m, block(source)], (d, q * k + (m + o) % k))
            for o in range(1, k)
        ]

    for copy in u_sent:
        copy.wait_recv()
    total = u_part[0]
    for i in range(1, nt):
        total = total + u_part[i]
    u[d] = total.astype(bf16)
    u_moved = [remote(u.at[d], u.at[d], (p, t)) for p in (p1, p2, p3)]

    for copy in squares_sent:
        copy.wait_recv()
    total = squares[0]
    for i in range(1, nt):
        total = total + squares[i]
    norm = jnp.sqrt(total + epsilon)
    scale = mag_ref[...] / norm

    keep_g.wait()
    swapped = {0: near(d)}
    x1.wait_recv()
    x2.wait_recv()
    for s, copy, p in zip((3, 1, 2), moved, (p3, p1, p2)):
        copy.wait_recv()
        swapped[s] = near(p)
    x3 = remote(x.at[block(p1, half)], x.at[block(p1, half)], (p2, t))
    x4 = remote(x.at[block(p2, half, half)], x.at[block(p2, half, half)], (p1, t))

    def share(s, p):
        for copy in swapped[s]:
            copy.wait_recv()
        at = block(p)
        for j in range(k):
            scaled[j, at] = (grad[j, at].astype(f32) * scale[:, j * nr:(j + 1) * nr]).astype(bf16)

        @pl.loop(0, n_tile)
        def _(i):
            cols = pl.ds(pl.multiple_of(i * width, width), width)
            acc = mm(scaled[0, at], w[0:nr, cols], 1, 0)
            for j in range(1, k):
                acc = acc + mm(scaled[j, at], w[j * nr:(j + 1) * nr, cols], 1, 0)
            if s:
                part[s - 1, :, cols] = acc.astype(bf16)
            else:
                own[:, cols] = acc

    low, high = pl.ds(0, half), pl.ds(half, half)
    share(3, p3)
    a1 = remote(part.at[2, low], got.at[0], (p1, t))
    b1 = remote(part.at[2, high], got.at[1], (p2, t))
    share(1, p1)
    a2 = remote(part.at[0, low], got.at[2], (p1, t))
    share(2, p2)
    b2 = remote(part.at[1, high], got.at[3], (p2, t))
    share(0, d)

    total = mm(upt_ref[:, 0:nr], scaled[0], 1, 1)
    for j in range(1, k):
        total = total + mm(upt_ref[:, j * nr:(j + 1) * nr], scaled[j], 1, 1)
    v[d] = total.astype(bf16)
    v_moved = [remote(v.at[d], v.at[d], (p, t)) for p in (p1, p2, p3)]

    def combine(copy, slot, index, at):
        copy.wait_recv()

        @pl.loop(0, n_tile)
        def _(i):
            cols = pl.ds(pl.multiple_of(i * width, width), width)
            part[index, at, cols] = (
                part[index, at, cols].astype(f32) + got[slot, :, cols].astype(f32)
            ).astype(bf16)

    x3.wait_recv()
    x4.wait_recv()

    def row_sums(j):
        @pl.loop(0, nr // side)
        def _(i):
            r = pl.ds(pl.multiple_of(j * nr + i * side, side), side)
            inner = pl.ds(pl.multiple_of(i * side, side), side)
            y = mm(x[...], w[r, :], 1, 1)
            sums[t, :, r] = jnp.sum(y * grad[j, :, inner].astype(f32), axis=0, keepdims=True)

    for j in range(k // 2):
        row_sums(j)
    combine(a1, 0, 1, low)
    a3 = remote(part.at[1, low], got.at[4], (p2, t))
    combine(b1, 1, 0, high)
    b3 = remote(part.at[0, high], got.at[5], (p1, t))
    for j in range(k // 2, k):
        row_sums(j)
    sums_sent = share_out(sums)

    for copy in u_moved:
        copy.wait_recv()
    for j in range(k):
        total = mm(u[0], grad[j, 0:tokens], 1, 0)
        for b in range(1, nd):
            total = total + mm(u[b], grad[j, b * tokens:(b + 1) * tokens], 1, 0)
        at = slice(j * nr, (j + 1) * nr)
        ug_ref[:, at] = adapter_scale * scale[:, at] * total

    for copy in v_moved:
        copy.wait_recv()
    total = v[0].astype(f32)
    for b in range(1, nd):
        total = total + v[b].astype(f32)
    v_all = total.astype(bf16)
    for c in range(n_tile):
        cols = slice(c * width, (c + 1) * width)
        dg_ref[:, cols] = adapter_scale * mm(v_all, x[:, cols], 1, 0)

    for copy in sums_sent:
        copy.wait_recv()
    total = sums[0]
    for i in range(1, nt):
        total = total + sums[i]
    mg_ref[...] = total / norm

    def finish(second, third, i2, i3, at):
        second.wait_recv()
        third.wait_recv()

        @pl.loop(0, n_tile)
        def _(i):
            cols = pl.ds(pl.multiple_of(i * width, width), width)
            dx_ref[at, cols] = (
                own[at, cols] + got[i2, :, cols].astype(f32) + got[i3, :, cols].astype(f32)
            ).astype(bf16)

    finish(a2, a3, 2, 4, low)
    finish(b2, b3, 3, 5, high)
    for copy in started:
        copy.wait_send()
    assert used[0] == n_local, used[0]


def local(inputs, output_gradient, frozen, down, up, magnitude):
    nd, nt = lax.axis_size("dp"), lax.axis_size("tensor")
    k = nt // nd
    tokens, columns = inputs.shape
    rows = frozen.shape[0]
    rank = down.shape[0]
    nr = output_gradient.shape[1]
    n_copies = 2 + (nd - 1) + 3 * (nt - 1) + 3 * 3 + nd * (k - 1) + 2 + 6
    anywhere = pl.BlockSpec(memory_space=pl.ANY)
    vmem = pl.BlockSpec(memory_space=pltpu.VMEM)
    half = tokens // 2
    dx, dg, ug, mg = pl.pallas_call(
        functools.partial(kernel, nd, nt, n_copies),
        out_shape=(
            jax.ShapeDtypeStruct((tokens, columns), bf16),
            jax.ShapeDtypeStruct((rank, columns), f32),
            jax.ShapeDtypeStruct((rank, rows), f32),
            jax.ShapeDtypeStruct((1, rows), f32),
        ),
        in_specs=[anywhere] * 3 + [vmem] * 4,
        out_specs=(vmem,) * 4,
        scratch_shapes=[
            pltpu.VMEM((rows, columns), bf16),
            pltpu.VMEM((nd * tokens, columns), bf16),
            pltpu.VMEM((nd, tokens, nr), bf16),
            pltpu.VMEM((k, nd * tokens, nr), bf16),
            pltpu.VMEM((k, nd * tokens, nr), bf16),
            pltpu.VMEM((3, tokens, columns), bf16),
            pltpu.VMEM((tokens, columns), f32),
            pltpu.VMEM((6, half, columns), bf16),
            pltpu.VMEM((nt, rank, tokens), f32),
            pltpu.VMEM((nd, rank, tokens), bf16),
            pltpu.VMEM((nd, rank, nd * tokens), bf16),
            pltpu.VMEM((nt, 1, rows), f32),
            pltpu.VMEM((nt, 1, rows), f32),
            pltpu.SemaphoreType.DMA((n_copies,)),
            pltpu.SemaphoreType.DMA((n_copies,)),
            pltpu.SemaphoreType.DMA((4,)),
        ],
        compiler_params=pltpu.CompilerParams(
            collective_id=0, has_side_effects=True, vmem_limit_bytes=62 * 1024 * 1024
        ),
    )(inputs, output_gradient, frozen, down, up, up.T, magnitude[None, :])
    return dx, dg, ug.T, mg[0]


def solution(mesh):
    placed = (
        P("dp", "tensor"),
        P("dp", "tensor"),
        P("dp", "tensor"),
        P(None, "tensor"),
        P("dp", None),
        P("dp"),
    )
    return jax.shard_map(
        local,
        mesh=mesh,
        in_specs=placed,
        out_specs=(P("dp", "tensor"), P(None, "tensor"), P("dp", None), P("dp")),
        check_vma=False,
    )
```

time: 325 us -> 180 us (0.55)
  waiting for transfers between devices: 173 us -> 0 us
  Pallas kernels: 0 us -> 171 us
  matrix products: 70.4 us -> 0 us
  blocking collectives: 34.7 us -> 0 us
  between operations: 15.5 us -> 0.66 us
  other arithmetic: 13 us -> 0 us
  starting transfers between devices: 10 us -> 0 us
    pallas_call x0 -> x1, Pallas kernels: none -> 171 us  [local(): pl.pallas_call(functools.partial(kernel, nd, nt, n_copies), out_shape=(ja...]
    all_gather x3 -> x0, waiting for transfers between devices: 98.8 us -> none  [the longest x1 52.4 us: local(): all_inputs = lax.all_gather(inputs, 'dp', axis=0, tiled=True)]
    dot_general x10 -> x0, matrix products: 70.4 us -> none  [mm(): lax.dot_general(a, b, (((ca,), (cb,)), ((), ())), preferred_element_type=...]
    psum x2 -> x0, waiting for transfers between devices: 28.2 us -> none  [the longest x1 17.6 us: local(): x_down = lax.psum(mm(inputs, down, 1, 1), 'tensor')]
    psum x1 -> x0, blocking collectives: 23.2 us -> none  [local(): squares = lax.psum(jnp.sum(merged * merged, axis=1), 'tensor')]
    all_to_all x1 -> x0, waiting for transfers between devices: 22.4 us -> none  [local(): part = lax.all_to_all(part, 'dp', split_axis=0, concat_axis=0)]
    ppermute x6 -> x0, waiting for transfers between devices: 22.1 us -> none  [swap(): return lax.ppermute(value, 'dp', [(i, i ^ s) for i in range(nd)])]
    all_gather x1 -> x0, blocking collectives: 11.5 us -> none  [local(): x_down = lax.all_gather(x_down, 'dp', axis=0, tiled=True)]
  transfers between devices with their start and end apart: 12 -> 0, of which waited for: 7 -> 0; matrix products, arithmetic and copies ran while one was open for 18% -> 0% of each run, Pallas kernels for 0% -> 0%
where the time goes in v2:
time: 180 us; the launch traced here: 179 us
  Pallas kernels  171 us (95%)
  local copies, waits for them, and re-layouts  7.24 us (4%)
    pallas_call x1, Pallas kernels, local(): pl.pallas_call(functools.partial(kernel, nd, nt, n_copies), out_shape=(ja...  171 us
    unnamed x11, local copies, waits for them, and re-layouts  7.24 us

profile of v2, /device:TPU:24, one launch (start us, length us, event | category | flops | bytes accessed | tf_op | source)
XLA Modules:
  0.0 179.0 jit_solution(15410463407259990697)
XLA Ops:
  0.6 2.0 %copy.10.up_ref = bf16[2048,64]{1,0:T(8,128)(2,1)} copy(bf16[2048,64]{0,1:T(8,128)(2,1)} %param.10) | data formatting | bytes 524288 | tf_op args[4]
  2.6 171.1 %shard_map.93 = (bf16[256,3584]{1,0:T(8,128)(2,1)}, f32[64,3584]{1,0:T(8,128)}, f32[64,2048]{1,0:T(8,128)}, f32[1,2048]{1,0:T(1,128)}) custom-call(bf16[256,3584]{1,0:T(8,128)(2,1)} %x_ref.1, bf16[256,1024]{1,0:T(8,128)(2,1)} %g_ref.1, bf16[2048,3584]{1,0:T(8,128)(2,1)} %w_ref.1, bf16[64,3584]{1,0:T(8,128)(2,1)} %down_ref.1, bf16[2048,64]{1,0:T(8,128)(2,1)} %copy.10.up_ref, ...), custom_call_target="tpu_custom_call" | custom-call | tf_op jit(solution)/shard_map/pallas_call | solution.py:259
  173.7 0.0 copy-start
  173.7 0.0 copy-start.1
  173.7 3.0 %copy.15 = bf16[256,3584]{1,0:T(8,128)(2,1)} copy(bf16[256,3584]{1,0:T(8,128)(2,1)} %get-tuple-element.16) | data formatting | bytes 3670016
  176.6 0.0 copy-done
  176.6 0.0 copy-start.2
  176.6 0.9 copy.16
  177.6 0.0 copy-done.1
  177.6 0.8 copy.17
  178.4 0.0 copy-done.2
  178.4 0.6 copy.18
Async XLA Ops:
  173.7 3.0 %copy-start = (f32[64,3584]{1,0:T(8,128)S(1)}, f32[64,3584]{1,0:T(8,128)}, u32[]{:S(2)}) copy-start(f32[64,3584]{1,0:T(8,128)} %get-tuple-element.17) | copy-start | bytes 2752516
  173.7 3.9 %copy-start.1 = (f32[64,2048]{1,0:T(8,128)S(1)}, f32[64,2048]{1,0:T(8,128)}, u32[]{:S(2)}) copy-start(f32[64,2048]{1,0:T(8,128)} %get-tuple-element.10) | copy-start | bytes 1572868
  176.6 1.7 copy-start.2

commit v3 on v2

--- a/solution.py
+++ b/solution.py
@@ -21,7 +21,7 @@
     nd, nt, n_local,
     x_ref, g_ref, w_ref, down_ref, up_ref, upt_ref, mag_ref,
     dx_ref, dg_ref, ug_ref, mg_ref,
-    w, x, gz, grad, scaled, part, own, got, u_part, u, v, squares, sums,
+    w, x, gz, grad, scaled, part, own, got, u_part, u, v, v_all, squares, sums,
     send, recv, local_sem,
 ):
     d, t = lax.axis_index("dp"), lax.axis_index("tensor")
@@ -76,7 +76,6 @@
 
     load_x.wait()
     u_part[t] = mm(down_ref[...], x[block(d)], 1, 1)
-    u_sent = share_out(u_part)
 
     load_w.wait()
 
@@ -103,20 +102,13 @@
     ]
     keep_g = pltpu.make_async_copy(gz.at[d], grad.at[m, block(d)], local_sem.at[3])
     keep_g.start()
+    u_sent = share_out(u_part)
 
     def near(source):
         return [
             remote(grad.at[m, block(source)], grad.at[m, block(source)], (d, q * k + (m + o) % k))
             for o in range(1, k)
         ]
-
-    for copy in u_sent:
-        copy.wait_recv()
-    total = u_part[0]
-    for i in range(1, nt):
-        total = total + u_part[i]
-    u[d] = total.astype(bf16)
-    u_moved = [remote(u.at[d], u.at[d], (p, t)) for p in (p1, p2, p3)]
 
     for copy in squares_sent:
         copy.wait_recv()
@@ -168,7 +160,16 @@
     for j in range(1, k):
         total = total + mm(upt_ref[:, j * nr:(j + 1) * nr], scaled[j], 1, 1)
     v[d] = total.astype(bf16)
-    v_moved = [remote(v.at[d], v.at[d], (p, t)) for p in (p1, p2, p3)]
+    lanes = pl.ds(pl.multiple_of(m * (nd * tokens // k), 128), nd * tokens // k)
+    v_moved = [remote(v.at[d, :, lanes], v.at[d, :, lanes], (p, t)) for p in (p1, p2, p3)]
+
+    for copy in u_sent:
+        copy.wait_recv()
+    total = u_part[0]
+    for i in range(1, nt):
+        total = total + u_part[i]
+    u[d] = total.astype(bf16)
+    u_moved = [remote(u.at[d], u.at[d], (p, t)) for p in (p1, p2, p3)]
 
     def combine(copy, slot, index, at):
         copy.wait_recv()
@@ -212,13 +213,19 @@
 
     for copy in v_moved:
         copy.wait_recv()
-    total = v[0].astype(f32)
+    total = v[0, :, lanes].astype(f32)
     for b in range(1, nd):
-        total = total + v[b].astype(f32)
-    v_all = total.astype(bf16)
+        total = total + v[b, :, lanes].astype(f32)
+    v_all[:, lanes] = total.astype(bf16)
+    v_near = [
+        remote(v_all.at[:, lanes], v_all.at[:, lanes], (d, q * k + (m + o) % k))
+        for o in range(1, k)
+    ]
+    for copy in v_near:
+        copy.wait_recv()
     for c in range(n_tile):
         cols = slice(c * width, (c + 1) * width)
-        dg_ref[:, cols] = adapter_scale * mm(v_all, x[:, cols], 1, 0)
+        dg_ref[:, cols] = adapter_scale * mm(v_all[...], x[:, cols], 1, 0)
 
     for copy in sums_sent:
         copy.wait_recv()
@@ -252,7 +259,7 @@
     rows = frozen.shape[0]
     rank = down.shape[0]
     nr = output_gradient.shape[1]
-    n_copies = 2 + (nd - 1) + 3 * (nt - 1) + 3 * 3 + nd * (k - 1) + 2 + 6
+    n_copies = 2 + (nd - 1) + 3 * (nt - 1) + 3 * 3 + (nd + 1) * (k - 1) + 2 + 6
     anywhere = pl.BlockSpec(memory_space=pl.ANY)
     vmem = pl.BlockSpec(memory_space=pltpu.VMEM)
     half = tokens // 2
@@ -278,6 +285,7 @@
             pltpu.VMEM((nt, rank, tokens), f32),
             pltpu.VMEM((nd, rank, tokens), bf16),
             pltpu.VMEM((nd, rank, nd * tokens), bf16),
+            pltpu.VMEM((rank, nd * tokens), bf16),
             pltpu.VMEM((nt, 1, rows), f32),
             pltpu.VMEM((nt, 1, rows), f32),
             pltpu.SemaphoreType.DMA((n_copies,)),

time: 180 us -> 177 us (0.983)
  Pallas kernels: 171 us -> 169 us
where the time goes in v3:
time: 177 us
  Pallas kernels  169 us (95%)
  local copies, waits for them, and re-layouts  7.24 us (4%)
    pallas_call x1, Pallas kernels, local(): pl.pallas_call(functools.partial(kernel, nd, nt, n_copies), out_shape=(ja...  169 us
    unnamed x11, local copies, waits for them, and re-layouts  7.24 us

profile of v3, /device:TPU:24, one launch (start us, length us, event | category | flops | bytes accessed | tf_op | source)
XLA Modules:
  0.0 177.2 jit_solution(10149230957601574022)
XLA Ops:
  0.6 2.0 %copy.10.up_ref = bf16[2048,64]{1,0:T(8,128)(2,1)} copy(bf16[2048,64]{0,1:T(8,128)(2,1)} %param.10) | data formatting | bytes 524288 | tf_op args[4]
  2.6 169.3 %shard_map.93 = (bf16[256,3584]{1,0:T(8,128)(2,1)}, f32[64,3584]{1,0:T(8,128)}, f32[64,2048]{1,0:T(8,128)}, f32[1,2048]{1,0:T(1,128)}) custom-call(bf16[256,3584]{1,0:T(8,128)(2,1)} %x_ref.1, bf16[256,1024]{1,0:T(8,128)(2,1)} %g_ref.1, bf16[2048,3584]{1,0:T(8,128)(2,1)} %w_ref.1, bf16[64,3584]{1,0:T(8,128)(2,1)} %down_ref.1, bf16[2048,64]{1,0:T(8,128)(2,1)} %copy.10.up_ref, ...), custom_call_target="tpu_custom_call" | custom-call | tf_op jit(solution)/shard_map/pallas_call | solution.py:266
  171.9 0.0 copy-start
  171.9 0.0 copy-start.1
  171.9 3.0 %copy.15 = bf16[256,3584]{1,0:T(8,128)(2,1)} copy(bf16[256,3584]{1,0:T(8,128)(2,1)} %get-tuple-element.16) | data formatting | bytes 3670016
  174.9 0.0 copy-done
  174.9 0.0 copy-start.2
  174.9 0.9 copy.16
  175.8 0.0 copy-done.1
  175.8 0.8 copy.17
  176.6 0.0 copy-done.2
  176.6 0.6 copy.18
Async XLA Ops:
  171.9 3.0 %copy-start = (f32[64,3584]{1,0:T(8,128)S(1)}, f32[64,3584]{1,0:T(8,128)}, u32[]{:S(2)}) copy-start(f32[64,3584]{1,0:T(8,128)} %get-tuple-element.17) | copy-start | bytes 2752516
  171.9 3.9 %copy-start.1 = (f32[64,2048]{1,0:T(8,128)S(1)}, f32[64,2048]{1,0:T(8,128)}, u32[]{:S(2)}) copy-start(f32[64,2048]{1,0:T(8,128)} %get-tuple-element.10) | copy-start | bytes 1572868
  174.9 1.7 copy-start.2
